TPU v7x, 512 devices: a whole 4x8x8 slice. The times are simulated.
512 devices in a mesh: group: 16 (over y, core), member: 32 (over x, z).
Axes of the slice: x: 4, y: 8, z: 8, core: 2. Of those that a mesh axis runs over, the one named last changes fastest.
Arguments:
- heads: bfloat16 [1048576, 768], P(('group', 'member')), may hold values from -16 to 16
- new_heads: bfloat16 [1024, 768], P('group'), may hold values from -16 to 16
- vectors: bfloat16 [512, 128, 768], P(('group', 'member')), may hold values from -16 to 16
- near_ids: int32 [512, 64], P(('group', 'member')), may hold values from 0 to 65535, as said below
Outputs:
- density: float32 [1024], P('group')
- spread: float32 [1024], P('group')
- reassign: float32 [512, 64, 128], P(('group', 'member'))
Inputs may be any that keep to these rules, and one draw needn't show every extreme that they name: `near_ids`: each row holds 64 different numbers; of one row at most 4 lie in one range j * 2048 to (j + 1) * 2048 - 1, and exactly 4 in some such range.
All inputs are finite; a program needn't handle non-finite values.
Results may differ from a plain program's by a relative error of at most 0.0003.
Values may be sent and summed in bfloat16 or wider, within the bound.
A program may use at most 64 MiB of HBM per device.

v0:
```python
import jax
import jax.numpy as jnp
from jax import lax
from jax.sharding import PartitionSpec as P


def passed_along(value, axis, steps):
    count = lax.axis_size(axis)
    pairs = [(source, (source + steps) % count) for source in range(count)]
    return lax.ppermute(value, axis, pairs)


def crowding(block, heads, head_sq, width):
    query_sq = jnp.sum(jnp.square(block.astype(jnp.float32)), axis=1)
    dots = lax.dot_general(
        block, heads, (((1,), (1,)), ((), ())), preferred_element_type=jnp.float32
    )
    excess = (query_sq[:, None] + head_sq[None, :] - 2.0 * dots) / width
    weight = 1.0 / jnp.square(1.0 + excess)
    return jnp.stack([jnp.sum(weight, axis=1), jnp.sum(weight * excess, axis=1)])


def distances(vec, rows, width):
    vec_sq = jnp.sum(jnp.square(vec.astype(jnp.float32)), axis=2)
    row_sq = jnp.sum(jnp.square(rows.astype(jnp.float32)), axis=2)
    dots = jnp.einsum("pbd,pkd->pkb", vec, rows, preferred_element_type=jnp.float32)
    return (row_sq[:, :, None] + vec_sq[:, None, :] - 2.0 * dots) / width


def per_device(heads, new_heads, vectors, near_ids):
    head_dev = heads.shape[0]
    width = heads.shape[1]
    groups = lax.axis_size("group")
    members = lax.axis_size("member")
    here = lax.axis_index("group")
    me = lax.axis_index("member")
    head_sq = jnp.sum(jnp.square(heads.astype(jnp.float32)), axis=1)
    new_count = new_heads.shape[0]
    table = jnp.zeros((groups, 2, new_count), jnp.float32)
    table = lax.dynamic_update_slice(
        table, crowding(new_heads, heads, head_sq, width)[None], (here, 0, 0)
    )

    def advance(step, carry):
        block, sums = carry
        block = passed_along(block, "group", 1)
        anchor = (here - step) % groups
        sums = lax.dynamic_update_slice(
            sums, crowding(block, heads, head_sq, width)[None], (anchor, 0, 0)
        )
        return (block, sums)

    unused, table = lax.fori_loop(1, groups, advance, (new_heads, table))
    mine = lax.psum_scatter(table, "group", scatter_dimension=0, tiled=True)
    mine = lax.psum(mine, "member")
    total_heads = float(head_dev * groups * members)
    density = jnp.log(mine[0, 0] / total_heads)
    spread = mine[0, 1] / mine[0, 0]
    lists = lax.all_gather(near_ids, "member", axis=0, tiled=True)
    blocks = lax.all_gather(vectors, "member", axis=0, tiled=True)
    owner = lists // head_dev
    local = lists % head_dev
    rows = jnp.take(heads, local, axis=0)
    rows, owned = (rows, owner == me)
    reassign = lax.psum_scatter(
        jnp.where(owned[:, :, None], distances(blocks, rows, width), 0.0),
        "member",
        scatter_dimension=0,
        tiled=True,
    )
    return (density, spread, reassign)


def solution(mesh):
    placed = (
        P(("group", "member"), None),
        P("group", None),
        P(("group", "member"), None, None),
        P(("group", "member"), None),
    )
    return jax.shard_map(
        per_device,
        mesh=mesh,
        in_specs=placed,
        out_specs=(P("group"), P("group"), P(("group", "member"), None, None)),
        check_vma=False,
    )
```

profile of v0, /device:TPU:32, one launch (start us, length us, event | category | flops | bytes accessed | tf_op | source)
XLA Modules:
  0.0 345.6 jit_solution(508991916548334194)
XLA Ops:
  7.2 0.9 copy.19
  8.2 44.1 %all-gather = s32[32,1,64]{2,1,0:T(1,128)S(1)} all-gather(s32[1,1,64]{2,1,0:T(1,128)} %bitcast.40), channel_id=1, replica_groups=mesh['group'=16,'member'=32] {'member'}, dimensions={0}, use_global_device_ids=true | all-gather | bytes 8448 | tf_op jit(solution)/shard_map/all_gather | solution.py:59
  52.4 1.3 dynamic-slice
  53.8 12.6 %gather_fusion = bf16[2048,768]{1,0:T(8,128)(2,1)} fusion(bf16[2048,768]{1,0:T(8,128)(2,1)} %param.6, s32[2048]{0:T(1024)S(1)} %broadcast_clamp_fusion), kind=kCustom, calls=%fused_computation | custom fusion | bytes 6299648 | tf_op jit(solution)/shard_map/jit(_take)/gather | solution.py:63
  66.3 0.1 multiply_reduce_fusion.6
  66.4 0.7 multiply_reduce_fusion.4
  67.1 1.2 fusion.10
  68.4 0.6 copy-done.1
  69.0 1.3 multiply_reduce_fusion.3
  70.4 39.8 %all-gather.3.cloned.1.call-done = bf16[32,128,768]{2,1,0:T(8,128)(2,1)} async-done(((bf16[1,128,768]{2,1,0:T(8,128)(2,1)}), bf16[32,128,768]{2,1,0:T(8,128)(2,1)}) %all-gather.3.cloned.1.call-update) | async-done | bytes 6291472 | tf_op jit(solution)/shard_map/all_gather | solution.py:60
  110.2 4.2 %multiply_reduce_fusion.2 = f32[32,128]{1,0:T(8,128)S(1)} fusion(bf16[32,128,768]{2,1,0:T(8,128)(2,1)} %all-gather.3.cloned.1.call-done), kind=kLoop, calls=%fused_computation.9 | loop fusion | flops 9433088 | bytes 6307840 | tf_op jit(solution)/shard_map/reduce_sum | solution.py:24
  114.4 5.3 %fusion.9 = f32[32,64,128]{2,1,0:T(8,128)} fusion(bf16[32,128,768]{2,1,0:T(8,128)(2,1)} %all-gather.3.cloned.1.call-done, bf16[32,64,768]{2,1,0:T(8,128)(2,1)S(1)} %bitcast.36, pred[32,64]{1,0:T(8,128)(4,1)S(1)} %get-tuple-element.175, f32[32,128]{1,0:T(8,128)S(1)} %multiply_reduce_fusion.2, f32[32,64]{1,0:T(8,128)S(1)} %multiply_reduce_fusion.3, ...), kind=kOutput, calls=%fused_computation.21 | convolution fusion | flops 405536768 | bytes 10514432 | tf_op jit(solution)/shard_map/pbd,pkd->pkb/dot_general | solution.py:26
  119.8 99.5 %while.17 = (s32[]{:T(128)}, bf16[64,768]{1,0:T(8,128)(2,1)S(1)}, f32[16,2,64]{2,1,0:T(2,128)S(1)}, f32[2048]{0:T(1024)S(1)}, bf16[2048,768]{1,0:T(8,128)(2,1)S(...) while((s32[]{:T(128)}, bf16[64,768]{1,0:T(8,128)(2,1)S(1)}, ...), condition=%wide.region_8.9_spmd, body=%wide.region_4.8_spmd.sunk | while | flops 202784720 | bytes 3943724 | solution.py:53
  119.8 5.2 %collective-permute-done = bf16[64,768]{1,0:T(8,128)(2,1)S(1)} collective-permute-done((bf16[64,768]{1,0:T(8,128)(2,1)S(1)}, bf16[64,768]{1,0:T(8,128)(2,1)S(1)}, u32[]{:S(2)}, u32[]{:S(2)}) %collective-permute-start) | collective-permute-done | bytes 98336 | tf_op jit(solution)/shard_map/while/body/eval_jaxpr/ppermute | solution.py:10
  125.0 0.1 multiply_reduce_fusion.8
  125.1 1.2 fusion.28
  126.4 5.2 %collective-permute-done = bf16[64,768]{1,0:T(8,128)(2,1)S(1)} collective-permute-done((bf16[64,768]{1,0:T(8,128)(2,1)S(1)}, bf16[64,768]{1,0:T(8,128)(2,1)S(1)}, u32[]{:S(2)}, u32[]{:S(2)}) %collective-permute-start) | collective-permute-done | bytes 98336 | tf_op jit(solution)/shard_map/while/body/eval_jaxpr/ppermute | solution.py:10
  131.8 1.2 fusion.28
  133.1 5.2 %collective-permute-done = bf16[64,768]{1,0:T(8,128)(2,1)S(1)} collective-permute-done((bf16[64,768]{1,0:T(8,128)(2,1)S(1)}, bf16[64,768]{1,0:T(8,128)(2,1)S(1)}, u32[]{:S(2)}, u32[]{:S(2)}) %collective-permute-start) | collective-permute-done | bytes 98336 | tf_op jit(solution)/shard_map/while/body/eval_jaxpr/ppermute | solution.py:10
  138.4 1.2 fusion.28
  139.7 5.2 %collective-permute-done = bf16[64,768]{1,0:T(8,128)(2,1)S(1)} collective-permute-done((bf16[64,768]{1,0:T(8,128)(2,1)S(1)}, bf16[64,768]{1,0:T(8,128)(2,1)S(1)}, u32[]{:S(2)}, u32[]{:S(2)}) %collective-permute-start) | collective-permute-done | bytes 98336 | tf_op jit(solution)/shard_map/while/body/eval_jaxpr/ppermute | solution.py:10
  145.0 1.2 fusion.28
  146.3 5.2 %collective-permute-done = bf16[64,768]{1,0:T(8,128)(2,1)S(1)} collective-permute-done((bf16[64,768]{1,0:T(8,128)(2,1)S(1)}, bf16[64,768]{1,0:T(8,128)(2,1)S(1)}, u32[]{:S(2)}, u32[]{:S(2)}) %collective-permute-start) | collective-permute-done | bytes 98336 | tf_op jit(solution)/shard_map/while/body/eval_jaxpr/ppermute | solution.py:10
  151.7 1.2 fusion.28
  153.0 5.2 %collective-permute-done = bf16[64,768]{1,0:T(8,128)(2,1)S(1)} collective-permute-done((bf16[64,768]{1,0:T(8,128)(2,1)S(1)}, bf16[64,768]{1,0:T(8,128)(2,1)S(1)}, u32[]{:S(2)}, u32[]{:S(2)}) %collective-permute-start) | collective-permute-done | bytes 98336 | tf_op jit(solution)/shard_map/while/body/eval_jaxpr/ppermute | solution.py:10
  158.3 1.2 fusion.28
  159.6 5.2 %collective-permute-done = bf16[64,768]{1,0:T(8,128)(2,1)S(1)} collective-permute-done((bf16[64,768]{1,0:T(8,128)(2,1)S(1)}, bf16[64,768]{1,0:T(8,128)(2,1)S(1)}, u32[]{:S(2)}, u32[]{:S(2)}) %collective-permute-start) | collective-permute-done | bytes 98336 | tf_op jit(solution)/shard_map/while/body/eval_jaxpr/ppermute | solution.py:10
  164.9 1.2 fusion.28
  166.2 5.2 %collective-permute-done = bf16[64,768]{1,0:T(8,128)(2,1)S(1)} collective-permute-done((bf16[64,768]{1,0:T(8,128)(2,1)S(1)}, bf16[64,768]{1,0:T(8,128)(2,1)S(1)}, u32[]{:S(2)}, u32[]{:S(2)}) %collective-permute-start) | collective-permute-done | bytes 98336 | tf_op jit(solution)/shard_map/while/body/eval_jaxpr/ppermute | solution.py:10
  171.6 1.2 fusion.28
  172.9 5.2 %collective-permute-done = bf16[64,768]{1,0:T(8,128)(2,1)S(1)} collective-permute-done((bf16[64,768]{1,0:T(8,128)(2,1)S(1)}, bf16[64,768]{1,0:T(8,128)(2,1)S(1)}, u32[]{:S(2)}, u32[]{:S(2)}) %collective-permute-start) | collective-permute-done | bytes 98336 | tf_op jit(solution)/shard_map/while/body/eval_jaxpr/ppermute | solution.py:10
  178.2 1.2 fusion.28
  179.5 5.2 %collective-permute-done = bf16[64,768]{1,0:T(8,128)(2,1)S(1)} collective-permute-done((bf16[64,768]{1,0:T(8,128)(2,1)S(1)}, bf16[64,768]{1,0:T(8,128)(2,1)S(1)}, u32[]{:S(2)}, u32[]{:S(2)}) %collective-permute-start) | collective-permute-done | bytes 98336 | tf_op jit(solution)/shard_map/while/body/eval_jaxpr/ppermute | solution.py:10
  184.8 1.2 fusion.28
  186.1 5.2 %collective-permute-done = bf16[64,768]{1,0:T(8,128)(2,1)S(1)} collective-permute-done((bf16[64,768]{1,0:T(8,128)(2,1)S(1)}, bf16[64,768]{1,0:T(8,128)(2,1)S(1)}, u32[]{:S(2)}, u32[]{:S(2)}) %collective-permute-start) | collective-permute-done | bytes 98336 | tf_op jit(solution)/shard_map/while/body/eval_jaxpr/ppermute | solution.py:10
  191.5 1.2 fusion.28
  192.8 5.2 %collective-permute-done = bf16[64,768]{1,0:T(8,128)(2,1)S(1)} collective-permute-done((bf16[64,768]{1,0:T(8,128)(2,1)S(1)}, bf16[64,768]{1,0:T(8,128)(2,1)S(1)}, u32[]{:S(2)}, u32[]{:S(2)}) %collective-permute-start) | collective-permute-done | bytes 98336 | tf_op jit(solution)/shard_map/while/body/eval_jaxpr/ppermute | solution.py:10
  198.1 1.2 fusion.28
  199.4 5.2 %collective-permute-done = bf16[64,768]{1,0:T(8,128)(2,1)S(1)} collective-permute-done((bf16[64,768]{1,0:T(8,128)(2,1)S(1)}, bf16[64,768]{1,0:T(8,128)(2,1)S(1)}, u32[]{:S(2)}, u32[]{:S(2)}) %collective-permute-start) | collective-permute-done | bytes 98336 | tf_op jit(solution)/shard_map/while/body/eval_jaxpr/ppermute | solution.py:10
  204.7 1.2 fusion.28
  206.0 5.2 %collective-permute-done = bf16[64,768]{1,0:T(8,128)(2,1)S(1)} collective-permute-done((bf16[64,768]{1,0:T(8,128)(2,1)S(1)}, bf16[64,768]{1,0:T(8,128)(2,1)S(1)}, u32[]{:S(2)}, u32[]{:S(2)}) %collective-permute-start) | collective-permute-done | bytes 98336 | tf_op jit(solution)/shard_map/while/body/eval_jaxpr/ppermute | solution.py:10
  211.4 1.2 fusion.28
  212.7 5.2 %collective-permute-done = bf16[64,768]{1,0:T(8,128)(2,1)S(1)} collective-permute-done((bf16[64,768]{1,0:T(8,128)(2,1)S(1)}, bf16[64,768]{1,0:T(8,128)(2,1)S(1)}, u32[]{:S(2)}, u32[]{:S(2)}) %collective-permute-start) | collective-permute-done | bytes 98336 | tf_op jit(solution)/shard_map/while/body/eval_jaxpr/ppermute | solution.py:10
  218.0 1.2 fusion.28
  219.3 46.5 %all-reduce = f32[16,2,64]{2,1,0:T(2,128)S(1)} all-reduce(f32[16,2,64]{2,1,0:T(2,128)S(1)} %get-tuple-element.158), channel_id=2, replica_groups=mesh['group'=16,'member'=32] {'group'}, use_global_device_ids=true, to_apply=%region_9.10.clone | all-reduce | flops 2048 | bytes 16384
  265.8 0.6 constant_dynamic-slice_fusion
  266.4 71.8 %psum.7 = f32[1,2,64]{2,1,0:T(2,128)S(1)} all-reduce(f32[1,2,64]{2,1,0:T(2,128)S(1)} %constant_dynamic-slice_fusion), channel_id=1, replica_groups=mesh['group'=16,'member'=32] {'member'}, use_global_device_ids=true, to_apply=%region_10.11 | all-reduce | flops 128 | bytes 1024 | tf_op jit(solution)/shard_map/psum | solution.py:55
  338.2 0.5 fusion.15
  (74 shorter events, 2.6 us)
Async XLA Ops:
  7.2 103.0 %all-gather.3.cloned.1.call-start = ((), (), s32[]{:S(2)}) async-start(), calls=%async_computation.1 | async-start | bytes 6488064 | tf_op jit(solution)/shard_map/all_gather | solution.py:60
  8.1 330.6 %reduce-scatter.2.cloned.1.call-start = ((), (), s32[]{:S(2)}) async-start(), calls=%async_computation.2 | async-start | bytes 1081344 | tf_op jit(solution)/shard_map/reduce_scatter | solution.py:65
  53.8 12.7 %copy-start = (bf16[2048,768]{1,0:T(8,128)(2,1)S(1)}, bf16[2048,768]{1,0:T(8,128)(2,1)}, u32[]{:S(2)}) copy-start(bf16[2048,768]{1,0:T(8,128)(2,1)} %param.6) | copy-start | bytes 9437188
  67.1 1.9 copy-start.1
  110.2 4.2 %copy-start.2 = (bf16[2048,768]{1,0:T(8,128)(2,1)S(1)}, bf16[2048,768]{1,0:T(8,128)(2,1)}, u32[]{:S(2)}) copy-start(bf16[2048,768]{1,0:T(8,128)(2,1)} %gather_fusion) | copy-start | bytes 9437188
  119.8 5.3 %collective-permute-start = (bf16[64,768]{1,0:T(8,128)(2,1)S(1)}, bf16[64,768]{1,0:T(8,128)(2,1)S(1)}, u32[]{:S(2)}, u32[]{:S(2)}) collective-permute-start(bf16[64,768]{1,0:T(8,128)(2,1)S(1)} %get-tuple-element.232), channel_id=1, source_target_pairs={{0,32},{32,64},{64,96},{96,128},{128,160},{160,192},{192,224},{224... | collective-permute-start | bytes 294920 | tf_op jit(solution)/shard_map/while/body/eval_jaxpr/ppermute | solution.py:10
  126.4 5.3 %collective-permute-start = (bf16[64,768]{1,0:T(8,128)(2,1)S(1)}, bf16[64,768]{1,0:T(8,128)(2,1)S(1)}, u32[]{:S(2)}, u32[]{:S(2)}) collective-permute-start(bf16[64,768]{1,0:T(8,128)(2,1)S(1)} %get-tuple-element.232), channel_id=1, source_target_pairs={{0,32},{32,64},{64,96},{96,128},{128,160},{160,192},{192,224},{224... | collective-permute-start | bytes 294920 | tf_op jit(solution)/shard_map/while/body/eval_jaxpr/ppermute | solution.py:10
  133.0 5.3 %collective-permute-start = (bf16[64,768]{1,0:T(8,128)(2,1)S(1)}, bf16[64,768]{1,0:T(8,128)(2,1)S(1)}, u32[]{:S(2)}, u32[]{:S(2)}) collective-permute-start(bf16[64,768]{1,0:T(8,128)(2,1)S(1)} %get-tuple-element.232), channel_id=1, source_target_pairs={{0,32},{32,64},{64,96},{96,128},{128,160},{160,192},{192,224},{224... | collective-permute-start | bytes 294920 | tf_op jit(solution)/shard_map/while/body/eval_jaxpr/ppermute | solution.py:10
  139.7 5.3 %collective-permute-start = (bf16[64,768]{1,0:T(8,128)(2,1)S(1)}, bf16[64,768]{1,0:T(8,128)(2,1)S(1)}, u32[]{:S(2)}, u32[]{:S(2)}) collective-permute-start(bf16[64,768]{1,0:T(8,128)(2,1)S(1)} %get-tuple-element.232), channel_id=1, source_target_pairs={{0,32},{32,64},{64,96},{96,128},{128,160},{160,192},{192,224},{224... | collective-permute-start | bytes 294920 | tf_op jit(solution)/shard_map/while/body/eval_jaxpr/ppermute | solution.py:10
  146.3 5.3 %collective-permute-start = (bf16[64,768]{1,0:T(8,128)(2,1)S(1)}, bf16[64,768]{1,0:T(8,128)(2,1)S(1)}, u32[]{:S(2)}, u32[]{:S(2)}) collective-permute-start(bf16[64,768]{1,0:T(8,128)(2,1)S(1)} %get-tuple-element.232), channel_id=1, source_target_pairs={{0,32},{32,64},{64,96},{96,128},{128,160},{160,192},{192,224},{224... | collective-permute-start | bytes 294920 | tf_op jit(solution)/shard_map/while/body/eval_jaxpr/ppermute | solution.py:10
  152.9 5.3 %collective-permute-start = (bf16[64,768]{1,0:T(8,128)(2,1)S(1)}, bf16[64,768]{1,0:T(8,128)(2,1)S(1)}, u32[]{:S(2)}, u32[]{:S(2)}) collective-permute-start(bf16[64,768]{1,0:T(8,128)(2,1)S(1)} %get-tuple-element.232), channel_id=1, source_target_pairs={{0,32},{32,64},{64,96},{96,128},{128,160},{160,192},{192,224},{224... | collective-permute-start | bytes 294920 | tf_op jit(solution)/shard_map/while/body/eval_jaxpr/ppermute | solution.py:10
  159.6 5.3 %collective-permute-start = (bf16[64,768]{1,0:T(8,128)(2,1)S(1)}, bf16[64,768]{1,0:T(8,128)(2,1)S(1)}, u32[]{:S(2)}, u32[]{:S(2)}) collective-permute-start(bf16[64,768]{1,0:T(8,128)(2,1)S(1)} %get-tuple-element.232), channel_id=1, source_target_pairs={{0,32},{32,64},{64,96},{96,128},{128,160},{160,192},{192,224},{224... | collective-permute-start | bytes 294920 | tf_op jit(solution)/shard_map/while/body/eval_jaxpr/ppermute | solution.py:10
  166.2 5.3 %collective-permute-start = (bf16[64,768]{1,0:T(8,128)(2,1)S(1)}, bf16[64,768]{1,0:T(8,128)(2,1)S(1)}, u32[]{:S(2)}, u32[]{:S(2)}) collective-permute-start(bf16[64,768]{1,0:T(8,128)(2,1)S(1)} %get-tuple-element.232), channel_id=1, source_target_pairs={{0,32},{32,64},{64,96},{96,128},{128,160},{160,192},{192,224},{224... | collective-permute-start | bytes 294920 | tf_op jit(solution)/shard_map/while/body/eval_jaxpr/ppermute | solution.py:10
  172.8 5.3 %collective-permute-start = (bf16[64,768]{1,0:T(8,128)(2,1)S(1)}, bf16[64,768]{1,0:T(8,128)(2,1)S(1)}, u32[]{:S(2)}, u32[]{:S(2)}) collective-permute-start(bf16[64,768]{1,0:T(8,128)(2,1)S(1)} %get-tuple-element.232), channel_id=1, source_target_pairs={{0,32},{32,64},{64,96},{96,128},{128,160},{160,192},{192,224},{224... | collective-permute-start | bytes 294920 | tf_op jit(solution)/shard_map/while/body/eval_jaxpr/ppermute | solution.py:10
  179.5 5.3 %collective-permute-start = (bf16[64,768]{1,0:T(8,128)(2,1)S(1)}, bf16[64,768]{1,0:T(8,128)(2,1)S(1)}, u32[]{:S(2)}, u32[]{:S(2)}) collective-permute-start(bf16[64,768]{1,0:T(8,128)(2,1)S(1)} %get-tuple-element.232), channel_id=1, source_target_pairs={{0,32},{32,64},{64,96},{96,128},{128,160},{160,192},{192,224},{224... | collective-permute-start | bytes 294920 | tf_op jit(solution)/shard_map/while/body/eval_jaxpr/ppermute | solution.py:10
  186.1 5.3 %collective-permute-start = (bf16[64,768]{1,0:T(8,128)(2,1)S(1)}, bf16[64,768]{1,0:T(8,128)(2,1)S(1)}, u32[]{:S(2)}, u32[]{:S(2)}) collective-permute-start(bf16[64,768]{1,0:T(8,128)(2,1)S(1)} %get-tuple-element.232), channel_id=1, source_target_pairs={{0,32},{32,64},{64,96},{96,128},{128,160},{160,192},{192,224},{224... | collective-permute-start | bytes 294920 | tf_op jit(solution)/shard_map/while/body/eval_jaxpr/ppermute | solution.py:10
  192.7 5.3 %collective-permute-start = (bf16[64,768]{1,0:T(8,128)(2,1)S(1)}, bf16[64,768]{1,0:T(8,128)(2,1)S(1)}, u32[]{:S(2)}, u32[]{:S(2)}) collective-permute-start(bf16[64,768]{1,0:T(8,128)(2,1)S(1)} %get-tuple-element.232), channel_id=1, source_target_pairs={{0,32},{32,64},{64,96},{96,128},{128,160},{160,192},{192,224},{224... | collective-permute-start | bytes 294920 | tf_op jit(solution)/shard_map/while/body/eval_jaxpr/ppermute | solution.py:10
  199.4 5.3 %collective-permute-start = (bf16[64,768]{1,0:T(8,128)(2,1)S(1)}, bf16[64,768]{1,0:T(8,128)(2,1)S(1)}, u32[]{:S(2)}, u32[]{:S(2)}) collective-permute-start(bf16[64,768]{1,0:T(8,128)(2,1)S(1)} %get-tuple-element.232), channel_id=1, source_target_pairs={{0,32},{32,64},{64,96},{96,128},{128,160},{160,192},{192,224},{224... | collective-permute-start | bytes 294920 | tf_op jit(solution)/shard_map/while/body/eval_jaxpr/ppermute | solution.py:10
  206.0 5.3 %collective-permute-start = (bf16[64,768]{1,0:T(8,128)(2,1)S(1)}, bf16[64,768]{1,0:T(8,128)(2,1)S(1)}, u32[]{:S(2)}, u32[]{:S(2)}) collective-permute-start(bf16[64,768]{1,0:T(8,128)(2,1)S(1)} %get-tuple-element.232), channel_id=1, source_target_pairs={{0,32},{32,64},{64,96},{96,128},{128,160},{160,192},{192,224},{224... | collective-permute-start | bytes 294920 | tf_op jit(solution)/shard_map/while/body/eval_jaxpr/ppermute | solution.py:10
  212.6 5.3 %collective-permute-start = (bf16[64,768]{1,0:T(8,128)(2,1)S(1)}, bf16[64,768]{1,0:T(8,128)(2,1)S(1)}, u32[]{:S(2)}, u32[]{:S(2)}) collective-permute-start(bf16[64,768]{1,0:T(8,128)(2,1)S(1)} %get-tuple-element.232), channel_id=1, source_target_pairs={{0,32},{32,64},{64,96},{96,128},{128,160},{160,192},{192,224},{224... | collective-permute-start | bytes 294920 | tf_op jit(solution)/shard_map/while/body/eval_jaxpr/ppermute | solution.py:10
Sparse Core Ops, SparseCore 0:
  11.2 98.9 all-gather.2
  119.9 217.1 reduce-scatter.1
where the time goes:
time: 346 us
  blocking collectives  162 us (47%)
  waiting for transfers between devices  118 us (34%)
  matrix products  24.4 us (7%)
  local copies, waits for them, and re-layouts  16.3 us (5%)
  between operations  14.1 us (4%)
  other arithmetic  9.04 us (3%)
    ppermute x15, waiting for transfers between devices, passed_along(): return lax.ppermute(value, axis, pairs)  78.2 us
    psum x1, blocking collectives, per_device(): mine = lax.psum(mine, 'member')  71.8 us
    unnamed x1, blocking collectives  46.5 us
    all_gather x1, blocking collectives, per_device(): lists = lax.all_gather(near_ids, 'member', axis=0, tiled=True)  44.1 us
    all_gather x1, waiting for transfers between devices, per_device(): blocks = lax.all_gather(vectors, 'member', axis=0, tiled=True)  39.8 us
    dot_general x16, matrix products, crowding(): lax.dot_general(block, heads, (((1,), (1,)), ((), ())), preferred_element...  19.2 us
    gather x1, local copies, waits for them, and re-layouts, per_device(): rows = jnp.take(heads, local, axis=0)  12.6 us
  transfers between devices with their start and end apart: 17, of which 16 were waited for; matrix products, arithmetic and copies ran while one was open for 11% of the time, Pallas kernels for 0%

commit v1 on v0

--- a/solution.py
+++ b/solution.py
@@ -52,7 +52,9 @@
 
     unused, table = lax.fori_loop(1, groups, advance, (new_heads, table))
     mine = lax.psum_scatter(table, "group", scatter_dimension=0, tiled=True)
-    mine = lax.psum(mine, "member")
+    mine = mine
+    for hop in (1, 2, 4, 8, 16):
+        mine = mine + lax.ppermute(mine, "member", [(dev, dev ^ hop) for dev in range(32)])
     total_heads = float(head_dev * groups * members)
     density = jnp.log(mine[0, 0] / total_heads)
     spread = mine[0, 1] / mine[0, 0]

time: 346 us -> 345 us (level)
  the two profiles are of different devices: /device:TPU:32 before, /device:TPU:8 now
where the time goes in v1:
time: 345 us; the launch traced here: 344 us
  waiting for transfers between devices  169 us (49%)
  blocking collectives  94.2 us (27%)
  matrix products  24.4 us (7%)
  local copies, waits for them, and re-layouts  16.3 us (5%)
  starting transfers between devices  15.5 us (4%)
  between operations  14.2 us (4%)
  other arithmetic  9.68 us (3%)
    ppermute x15, waiting for transfers between devices, passed_along(): return lax.ppermute(value, axis, pairs)  71.5 us
    unnamed x1, blocking collectives  50 us
    all_gather x1, blocking collectives, per_device(): lists = lax.all_gather(near_ids, 'member', axis=0, tiled=True)  44.2 us
    all_gather x1, waiting for transfers between devices, per_device(): blocks = lax.all_gather(vectors, 'member', axis=0, tiled=True)  40.1 us
    reduce_scatter x1, waiting for transfers between devices, per_device(): lax.psum_scatter(jnp.where(owned[:, :, None], distances(blocks, rows, wid...  39.2 us
    dot_general x16, matrix products, crowding(): lax.dot_general(block, heads, (((1,), (1,)), ((), ())), preferred_element...  19.1 us
    ppermute x5, waiting for transfers between devices, per_device(): lax.ppermute(mine, 'member', [(dev, dev ^ hop) for dev in range(32)])  18.4 us
    ppermute x5, starting transfers between devices, per_device(): lax.ppermute(mine, 'member', [(dev, dev ^ hop) for dev in range(32)])  15.2 us
  transfers between devices with their start and end apart: 22, of which 22 were waited for; matrix products, arithmetic and copies ran while one was open for 11% of the time, Pallas kernels for 0%

profile of v1, /device:TPU:8, one launch (start us, length us, event | category | flops | bytes accessed | tf_op | source)
XLA Modules:
  0.0 344.2 jit_solution(3698289854586114317)
XLA Ops:
  8.2 44.2 %all-gather = s32[32,1,64]{2,1,0:T(1,128)S(1)} all-gather(s32[1,1,64]{2,1,0:T(1,128)} %bitcast.40), channel_id=1, replica_groups=mesh['group'=16,'member'=32] {'member'}, dimensions={0}, use_global_device_ids=true | all-gather | bytes 8448 | tf_op jit(solution)/shard_map/all_gather | solution.py:61
  52.4 1.3 dynamic-slice
  53.8 12.6 %gather_fusion = bf16[2048,768]{1,0:T(8,128)(2,1)} fusion(bf16[2048,768]{1,0:T(8,128)(2,1)} %param.6, s32[2048]{0:T(1024)S(1)} %broadcast_clamp_fusion), kind=kCustom, calls=%fused_computation | custom fusion | bytes 6299648 | tf_op jit(solution)/shard_map/jit(_take)/gather | solution.py:65
  67.2 1.2 fusion.10
  69.0 1.3 multiply_reduce_fusion.3
  70.4 40.1 %all-gather.3.cloned.1.call-done = bf16[32,128,768]{2,1,0:T(8,128)(2,1)} async-done(((bf16[1,128,768]{2,1,0:T(8,128)(2,1)}), bf16[32,128,768]{2,1,0:T(8,128)(2,1)}) %all-gather.3.cloned.1.call-update) | async-done | bytes 6291472 | tf_op jit(solution)/shard_map/all_gather | solution.py:62
  110.5 4.2 %multiply_reduce_fusion.2 = f32[32,128]{1,0:T(8,128)S(1)} fusion(bf16[32,128,768]{2,1,0:T(8,128)(2,1)} %all-gather.3.cloned.1.call-done), kind=kLoop, calls=%fused_computation.9 | loop fusion | flops 9433088 | bytes 6307840 | tf_op jit(solution)/shard_map/reduce_sum | solution.py:24
  114.7 5.3 %fusion.9 = f32[32,64,128]{2,1,0:T(8,128)} fusion(bf16[32,128,768]{2,1,0:T(8,128)(2,1)} %all-gather.3.cloned.1.call-done, bf16[32,64,768]{2,1,0:T(8,128)(2,1)S(1)} %bitcast.36, pred[32,64]{1,0:T(8,128)(4,1)S(1)} %get-tuple-element.175, f32[32,128]{1,0:T(8,128)S(1)} %multiply_reduce_fusion.2, f32[32,64]{1,0:T(8,128)S(1)} %multiply_reduce_fusion.3, ...), kind=kOutput, calls=%fused_computation.21 | convolution fusion | flops 405536768 | bytes 10514432 | tf_op jit(solution)/shard_map/pbd,pkd->pkb/dot_general | solution.py:26
  120.0 92.7 %while.17 = (s32[]{:T(128)}, bf16[64,768]{1,0:T(8,128)(2,1)S(1)}, f32[16,2,64]{2,1,0:T(2,128)S(1)}, f32[2048]{0:T(1024)S(1)}, bf16[2048,768]{1,0:T(8,128)(2,1)S(...) while((s32[]{:T(128)}, bf16[64,768]{1,0:T(8,128)(2,1)S(1)}, ...), condition=%wide.region_8.9_spmd, body=%wide.region_4.8_spmd.sunk | while | flops 202784720 | bytes 3943724 | solution.py:53
  120.1 4.0 %collective-permute-done = bf16[64,768]{1,0:T(8,128)(2,1)S(1)} collective-permute-done((bf16[64,768]{1,0:T(8,128)(2,1)S(1)}, bf16[64,768]{1,0:T(8,128)(2,1)S(1)}, u32[]{:S(2)}, u32[]{:S(2)}) %collective-permute-start) | collective-permute-done | bytes 98336 | tf_op jit(solution)/shard_map/while/body/eval_jaxpr/ppermute | solution.py:10
  124.2 1.2 fusion.29
  125.5 4.0 %collective-permute-done = bf16[64,768]{1,0:T(8,128)(2,1)S(1)} collective-permute-done((bf16[64,768]{1,0:T(8,128)(2,1)S(1)}, bf16[64,768]{1,0:T(8,128)(2,1)S(1)}, u32[]{:S(2)}, u32[]{:S(2)}) %collective-permute-start) | collective-permute-done | bytes 98336 | tf_op jit(solution)/shard_map/while/body/eval_jaxpr/ppermute | solution.py:10
  129.6 1.2 fusion.29
  130.9 4.0 %collective-permute-done = bf16[64,768]{1,0:T(8,128)(2,1)S(1)} collective-permute-done((bf16[64,768]{1,0:T(8,128)(2,1)S(1)}, bf16[64,768]{1,0:T(8,128)(2,1)S(1)}, u32[]{:S(2)}, u32[]{:S(2)}) %collective-permute-start) | collective-permute-done | bytes 98336 | tf_op jit(solution)/shard_map/while/body/eval_jaxpr/ppermute | solution.py:10
  135.1 1.2 fusion.29
  136.4 4.0 %collective-permute-done = bf16[64,768]{1,0:T(8,128)(2,1)S(1)} collective-permute-done((bf16[64,768]{1,0:T(8,128)(2,1)S(1)}, bf16[64,768]{1,0:T(8,128)(2,1)S(1)}, u32[]{:S(2)}, u32[]{:S(2)}) %collective-permute-start) | collective-permute-done | bytes 98336 | tf_op jit(solution)/shard_map/while/body/eval_jaxpr/ppermute | solution.py:10
  140.5 1.2 fusion.29
  141.8 4.0 %collective-permute-done = bf16[64,768]{1,0:T(8,128)(2,1)S(1)} collective-permute-done((bf16[64,768]{1,0:T(8,128)(2,1)S(1)}, bf16[64,768]{1,0:T(8,128)(2,1)S(1)}, u32[]{:S(2)}, u32[]{:S(2)}) %collective-permute-start) | collective-permute-done | bytes 98336 | tf_op jit(solution)/shard_map/while/body/eval_jaxpr/ppermute | solution.py:10
  145.9 1.2 fusion.29
  147.2 4.5 %collective-permute-done = bf16[64,768]{1,0:T(8,128)(2,1)S(1)} collective-permute-done((bf16[64,768]{1,0:T(8,128)(2,1)S(1)}, bf16[64,768]{1,0:T(8,128)(2,1)S(1)}, u32[]{:S(2)}, u32[]{:S(2)}) %collective-permute-start) | collective-permute-done | bytes 98336 | tf_op jit(solution)/shard_map/while/body/eval_jaxpr/ppermute | solution.py:10
  151.8 1.2 fusion.29
  153.1 5.2 %collective-permute-done = bf16[64,768]{1,0:T(8,128)(2,1)S(1)} collective-permute-done((bf16[64,768]{1,0:T(8,128)(2,1)S(1)}, bf16[64,768]{1,0:T(8,128)(2,1)S(1)}, u32[]{:S(2)}, u32[]{:S(2)}) %collective-permute-start) | collective-permute-done | bytes 98336 | tf_op jit(solution)/shard_map/while/body/eval_jaxpr/ppermute | solution.py:10
  158.5 1.2 fusion.29
  159.8 5.2 %collective-permute-done = bf16[64,768]{1,0:T(8,128)(2,1)S(1)} collective-permute-done((bf16[64,768]{1,0:T(8,128)(2,1)S(1)}, bf16[64,768]{1,0:T(8,128)(2,1)S(1)}, u32[]{:S(2)}, u32[]{:S(2)}) %collective-permute-start) | collective-permute-done | bytes 98336 | tf_op jit(solution)/shard_map/while/body/eval_jaxpr/ppermute | solution.py:10
  166.4 5.2 %collective-permute-done = bf16[64,768]{1,0:T(8,128)(2,1)S(1)} collective-permute-done((bf16[64,768]{1,0:T(8,128)(2,1)S(1)}, bf16[64,768]{1,0:T(8,128)(2,1)S(1)}, u32[]{:S(2)}, u32[]{:S(2)}) %collective-permute-start) | collective-permute-done | bytes 98336 | tf_op jit(solution)/shard_map/while/body/eval_jaxpr/ppermute | solution.py:10
  171.7 1.2 fusion.29
  173.0 5.2 %collective-permute-done = bf16[64,768]{1,0:T(8,128)(2,1)S(1)} collective-permute-done((bf16[64,768]{1,0:T(8,128)(2,1)S(1)}, bf16[64,768]{1,0:T(8,128)(2,1)S(1)}, u32[]{:S(2)}, u32[]{:S(2)}) %collective-permute-start) | collective-permute-done | bytes 98336 | tf_op jit(solution)/shard_map/while/body/eval_jaxpr/ppermute | solution.py:10
  178.4 1.2 fusion.29
  179.7 5.2 %collective-permute-done = bf16[64,768]{1,0:T(8,128)(2,1)S(1)} collective-permute-done((bf16[64,768]{1,0:T(8,128)(2,1)S(1)}, bf16[64,768]{1,0:T(8,128)(2,1)S(1)}, u32[]{:S(2)}, u32[]{:S(2)}) %collective-permute-start) | collective-permute-done | bytes 98336 | tf_op jit(solution)/shard_map/while/body/eval_jaxpr/ppermute | solution.py:10
  185.0 1.2 fusion.29
  186.3 5.2 %collective-permute-done = bf16[64,768]{1,0:T(8,128)(2,1)S(1)} collective-permute-done((bf16[64,768]{1,0:T(8,128)(2,1)S(1)}, bf16[64,768]{1,0:T(8,128)(2,1)S(1)}, u32[]{:S(2)}, u32[]{:S(2)}) %collective-permute-start) | collective-permute-done | bytes 98336 | tf_op jit(solution)/shard_map/while/body/eval_jaxpr/ppermute | solution.py:10
  192.9 5.2 %collective-permute-done = bf16[64,768]{1,0:T(8,128)(2,1)S(1)} collective-permute-done((bf16[64,768]{1,0:T(8,128)(2,1)S(1)}, bf16[64,768]{1,0:T(8,128)(2,1)S(1)}, u32[]{:S(2)}, u32[]{:S(2)}) %collective-permute-start) | collective-permute-done | bytes 98336 | tf_op jit(solution)/shard_map/while/body/eval_jaxpr/ppermute | solution.py:10
  198.3 1.2 fusion.29
  199.6 5.2 %collective-permute-done = bf16[64,768]{1,0:T(8,128)(2,1)S(1)} collective-permute-done((bf16[64,768]{1,0:T(8,128)(2,1)S(1)}, bf16[64,768]{1,0:T(8,128)(2,1)S(1)}, u32[]{:S(2)}, u32[]{:S(2)}) %collective-permute-start) | collective-permute-done | bytes 98336 | tf_op jit(solution)/shard_map/while/body/eval_jaxpr/ppermute | solution.py:10
  206.2 5.2 %collective-permute-done = bf16[64,768]{1,0:T(8,128)(2,1)S(1)} collective-permute-done((bf16[64,768]{1,0:T(8,128)(2,1)S(1)}, bf16[64,768]{1,0:T(8,128)(2,1)S(1)}, u32[]{:S(2)}, u32[]{:S(2)}) %collective-permute-start) | collective-permute-done | bytes 98336 | tf_op jit(solution)/shard_map/while/body/eval_jaxpr/ppermute | solution.py:10
  211.5 1.2 fusion.29
  212.8 50.0 %all-reduce = f32[16,2,64]{2,1,0:T(2,128)S(1)} all-reduce(f32[16,2,64]{2,1,0:T(2,128)S(1)} %get-tuple-element.158), channel_id=2, replica_groups=mesh['group'=16,'member'=32] {'group'}, use_global_device_ids=true, to_apply=%region_9.10.clone | all-reduce | flops 2048 | bytes 16384
  263.4 3.1 collective-permute-start.1
  266.6 2.3 collective-permute-done.1
  269.5 2.9 collective-permute-start.2
  272.4 3.5 %collective-permute-done.2 = f32[1,2,64]{2,1,0:T(2,128)S(1)} collective-permute-done((f32[1,2,64]{2,1,0:T(2,128)S(1)}, f32[1,2,64]{2,1,0:T(2,128)S(1)}, u32[]{:S(2)}, u32[]{:S(2)}) %collective-permute-start.2) | collective-permute-done | bytes 544 | tf_op jit(solution)/shard_map/ppermute | solution.py:57
  275.9 4.3 %collective-permute-start.3 = (f32[1,2,64]{2,1,0:T(2,128)S(1)}, f32[1,2,64]{2,1,0:T(2,128)S(1)}, u32[]{:S(2)}, u32[]{:S(2)}) collective-permute-start(f32[1,2,64]{2,1,0:T(2,128)S(1)} %add.163), channel_id=1, source_target_pairs={{0,4},{1,5},{2,6},{3,7},{4,0},{5,1},{6,2},{7,3},{8,12},{9,13},{10,... | collective-permute-start | bytes 1544 | tf_op jit(solution)/shard_map/ppermute | solution.py:57
  280.2 5.0 %collective-permute-done.3 = f32[1,2,64]{2,1,0:T(2,128)S(1)} collective-permute-done((f32[1,2,64]{2,1,0:T(2,128)S(1)}, f32[1,2,64]{2,1,0:T(2,128)S(1)}, u32[]{:S(2)}, u32[]{:S(2)}) %collective-permute-start.3) | collective-permute-done | bytes 544 | tf_op jit(solution)/shard_map/ppermute | solution.py:57
  285.2 1.9 collective-permute-start.4
  287.2 3.5 %collective-permute-done.4 = f32[1,2,64]{2,1,0:T(2,128)S(1)} collective-permute-done((f32[1,2,64]{2,1,0:T(2,128)S(1)}, f32[1,2,64]{2,1,0:T(2,128)S(1)}, u32[]{:S(2)}, u32[]{:S(2)}) %collective-permute-start.4) | collective-permute-done | bytes 544 | tf_op jit(solution)/shard_map/ppermute | solution.py:57
  290.7 3.0 collective-permute-start.5
  293.7 4.0 %collective-permute-done.5 = f32[1,2,64]{2,1,0:T(2,128)S(1)} collective-permute-done((f32[1,2,64]{2,1,0:T(2,128)S(1)}, f32[1,2,64]{2,1,0:T(2,128)S(1)}, u32[]{:S(2)}, u32[]{:S(2)}) %collective-permute-start.5) | collective-permute-done | bytes 544 | tf_op jit(solution)/shard_map/ppermute | solution.py:57
  298.2 39.2 %reduce-scatter.2.cloned.1.call-done = f32[1,64,128]{2,1,0:T(8,128)} async-done(((f32[32,64,128]{2,1,0:T(8,128)}), f32[1,64,128]{2,1,0:T(8,128)}) %reduce-scatter.2.cloned.1.call-update) | async-done | bytes 32784 | tf_op jit(solution)/shard_map/reduce_scatter | solution.py:67
  (88 shorter events, 10.5 us)
Async XLA Ops:
  7.2 103.3 %all-gather.3.cloned.1.call-start = ((), (), s32[]{:S(2)}) async-start(), calls=%async_computation.1 | async-start | bytes 6488064 | tf_op jit(solution)/shard_map/all_gather | solution.py:62
  8.1 329.2 %reduce-scatter.2.cloned.1.call-start = ((), (), s32[]{:S(2)}) async-start(), calls=%async_computation.2 | async-start | bytes 1081344 | tf_op jit(solution)/shard_map/reduce_scatter | solution.py:67
  53.8 12.7 %copy-start = (bf16[2048,768]{1,0:T(8,128)(2,1)S(1)}, bf16[2048,768]{1,0:T(8,128)(2,1)}, u32[]{:S(2)}) copy-start(bf16[2048,768]{1,0:T(8,128)(2,1)} %param.6) | copy-start | bytes 9437188
  67.1 1.9 copy-start.1
  110.5 4.2 %copy-start.2 = (bf16[2048,768]{1,0:T(8,128)(2,1)S(1)}, bf16[2048,768]{1,0:T(8,128)(2,1)}, u32[]{:S(2)}) copy-start(bf16[2048,768]{1,0:T(8,128)(2,1)} %gather_fusion) | copy-start | bytes 9437188
  120.0 4.1 %collective-permute-start = (bf16[64,768]{1,0:T(8,128)(2,1)S(1)}, bf16[64,768]{1,0:T(8,128)(2,1)S(1)}, u32[]{:S(2)}, u32[]{:S(2)}) collective-permute-start(bf16[64,768]{1,0:T(8,128)(2,1)S(1)} %get-tuple-element.232), channel_id=1, source_target_pairs={{0,32},{32,64},{64,96},{96,128},{128,160},{160,192},{192,224},{224... | collective-permute-start | bytes 294920 | tf_op jit(solution)/shard_map/while/body/eval_jaxpr/ppermute | solution.py:10
  125.5 4.1 %collective-permute-start = (bf16[64,768]{1,0:T(8,128)(2,1)S(1)}, bf16[64,768]{1,0:T(8,128)(2,1)S(1)}, u32[]{:S(2)}, u32[]{:S(2)}) collective-permute-start(bf16[64,768]{1,0:T(8,128)(2,1)S(1)} %get-tuple-element.232), channel_id=1, source_target_pairs={{0,32},{32,64},{64,96},{96,128},{128,160},{160,192},{192,224},{224... | collective-permute-start | bytes 294920 | tf_op jit(solution)/shard_map/while/body/eval_jaxpr/ppermute | solution.py:10
  130.9 4.1 %collective-permute-start = (bf16[64,768]{1,0:T(8,128)(2,1)S(1)}, bf16[64,768]{1,0:T(8,128)(2,1)S(1)}, u32[]{:S(2)}, u32[]{:S(2)}) collective-permute-start(bf16[64,768]{1,0:T(8,128)(2,1)S(1)} %get-tuple-element.232), channel_id=1, source_target_pairs={{0,32},{32,64},{64,96},{96,128},{128,160},{160,192},{192,224},{224... | collective-permute-start | bytes 294920 | tf_op jit(solution)/shard_map/while/body/eval_jaxpr/ppermute | solution.py:10
  136.3 4.1 %collective-permute-start = (bf16[64,768]{1,0:T(8,128)(2,1)S(1)}, bf16[64,768]{1,0:T(8,128)(2,1)S(1)}, u32[]{:S(2)}, u32[]{:S(2)}) collective-permute-start(bf16[64,768]{1,0:T(8,128)(2,1)S(1)} %get-tuple-element.232), channel_id=1, source_target_pairs={{0,32},{32,64},{64,96},{96,128},{128,160},{160,192},{192,224},{224... | collective-permute-start | bytes 294920 | tf_op jit(solution)/shard_map/while/body/eval_jaxpr/ppermute | solution.py:10
  141.7 4.1 %collective-permute-start = (bf16[64,768]{1,0:T(8,128)(2,1)S(1)}, bf16[64,768]{1,0:T(8,128)(2,1)S(1)}, u32[]{:S(2)}, u32[]{:S(2)}) collective-permute-start(bf16[64,768]{1,0:T(8,128)(2,1)S(1)} %get-tuple-element.232), channel_id=1, source_target_pairs={{0,32},{32,64},{64,96},{96,128},{128,160},{160,192},{192,224},{224... | collective-permute-start | bytes 294920 | tf_op jit(solution)/shard_map/while/body/eval_jaxpr/ppermute | solution.py:10
  147.2 4.6 %collective-permute-start = (bf16[64,768]{1,0:T(8,128)(2,1)S(1)}, bf16[64,768]{1,0:T(8,128)(2,1)S(1)}, u32[]{:S(2)}, u32[]{:S(2)}) collective-permute-start(bf16[64,768]{1,0:T(8,128)(2,1)S(1)} %get-tuple-element.232), channel_id=1, source_target_pairs={{0,32},{32,64},{64,96},{96,128},{128,160},{160,192},{192,224},{224... | collective-permute-start | bytes 294920 | tf_op jit(solution)/shard_map/while/body/eval_jaxpr/ppermute | solution.py:10
  153.1 5.3 %collective-permute-start = (bf16[64,768]{1,0:T(8,128)(2,1)S(1)}, bf16[64,768]{1,0:T(8,128)(2,1)S(1)}, u32[]{:S(2)}, u32[]{:S(2)}) collective-permute-start(bf16[64,768]{1,0:T(8,128)(2,1)S(1)} %get-tuple-element.232), channel_id=1, source_target_pairs={{0,32},{32,64},{64,96},{96,128},{128,160},{160,192},{192,224},{224... | collective-permute-start | bytes 294920 | tf_op jit(solution)/shard_map/while/body/eval_jaxpr/ppermute | solution.py:10
  159.7 5.3 %collective-permute-start = (bf16[64,768]{1,0:T(8,128)(2,1)S(1)}, bf16[64,768]{1,0:T(8,128)(2,1)S(1)}, u32[]{:S(2)}, u32[]{:S(2)}) collective-permute-start(bf16[64,768]{1,0:T(8,128)(2,1)S(1)} %get-tuple-element.232), channel_id=1, source_target_pairs={{0,32},{32,64},{64,96},{96,128},{128,160},{160,192},{192,224},{224... | collective-permute-start | bytes 294920 | tf_op jit(solution)/shard_map/while/body/eval_jaxpr/ppermute | solution.py:10
  166.3 5.3 %collective-permute-start = (bf16[64,768]{1,0:T(8,128)(2,1)S(1)}, bf16[64,768]{1,0:T(8,128)(2,1)S(1)}, u32[]{:S(2)}, u32[]{:S(2)}) collective-permute-start(bf16[64,768]{1,0:T(8,128)(2,1)S(1)} %get-tuple-element.232), channel_id=1, source_target_pairs={{0,32},{32,64},{64,96},{96,128},{128,160},{160,192},{192,224},{224... | collective-permute-start | bytes 294920 | tf_op jit(solution)/shard_map/while/body/eval_jaxpr/ppermute | solution.py:10
  173.0 5.3 %collective-permute-start = (bf16[64,768]{1,0:T(8,128)(2,1)S(1)}, bf16[64,768]{1,0:T(8,128)(2,1)S(1)}, u32[]{:S(2)}, u32[]{:S(2)}) collective-permute-start(bf16[64,768]{1,0:T(8,128)(2,1)S(1)} %get-tuple-element.232), channel_id=1, source_target_pairs={{0,32},{32,64},{64,96},{96,128},{128,160},{160,192},{192,224},{224... | collective-permute-start | bytes 294920 | tf_op jit(solution)/shard_map/while/body/eval_jaxpr/ppermute | solution.py:10
  179.6 5.3 %collective-permute-start = (bf16[64,768]{1,0:T(8,128)(2,1)S(1)}, bf16[64,768]{1,0:T(8,128)(2,1)S(1)}, u32[]{:S(2)}, u32[]{:S(2)}) collective-permute-start(bf16[64,768]{1,0:T(8,128)(2,1)S(1)} %get-tuple-element.232), channel_id=1, source_target_pairs={{0,32},{32,64},{64,96},{96,128},{128,160},{160,192},{192,224},{224... | collective-permute-start | bytes 294920 | tf_op jit(solution)/shard_map/while/body/eval_jaxpr/ppermute | solution.py:10
  186.2 5.3 %collective-permute-start = (bf16[64,768]{1,0:T(8,128)(2,1)S(1)}, bf16[64,768]{1,0:T(8,128)(2,1)S(1)}, u32[]{:S(2)}, u32[]{:S(2)}) collective-permute-start(bf16[64,768]{1,0:T(8,128)(2,1)S(1)} %get-tuple-element.232), channel_id=1, source_target_pairs={{0,32},{32,64},{64,96},{96,128},{128,160},{160,192},{192,224},{224... | collective-permute-start | bytes 294920 | tf_op jit(solution)/shard_map/while/body/eval_jaxpr/ppermute | solution.py:10
  192.9 5.3 %collective-permute-start = (bf16[64,768]{1,0:T(8,128)(2,1)S(1)}, bf16[64,768]{1,0:T(8,128)(2,1)S(1)}, u32[]{:S(2)}, u32[]{:S(2)}) collective-permute-start(bf16[64,768]{1,0:T(8,128)(2,1)S(1)} %get-tuple-element.232), channel_id=1, source_target_pairs={{0,32},{32,64},{64,96},{96,128},{128,160},{160,192},{192,224},{224... | collective-permute-start | bytes 294920 | tf_op jit(solution)/shard_map/while/body/eval_jaxpr/ppermute | solution.py:10
  199.5 5.3 %collective-permute-start = (bf16[64,768]{1,0:T(8,128)(2,1)S(1)}, bf16[64,768]{1,0:T(8,128)(2,1)S(1)}, u32[]{:S(2)}, u32[]{:S(2)}) collective-permute-start(bf16[64,768]{1,0:T(8,128)(2,1)S(1)} %get-tuple-element.232), channel_id=1, source_target_pairs={{0,32},{32,64},{64,96},{96,128},{128,160},{160,192},{192,224},{224... | collective-permute-start | bytes 294920 | tf_op jit(solution)/shard_map/while/body/eval_jaxpr/ppermute | solution.py:10
  206.1 5.3 %collective-permute-start = (bf16[64,768]{1,0:T(8,128)(2,1)S(1)}, bf16[64,768]{1,0:T(8,128)(2,1)S(1)}, u32[]{:S(2)}, u32[]{:S(2)}) collective-permute-start(bf16[64,768]{1,0:T(8,128)(2,1)S(1)} %get-tuple-element.232), channel_id=1, source_target_pairs={{0,32},{32,64},{64,96},{96,128},{128,160},{160,192},{192,224},{224... | collective-permute-start | bytes 294920 | tf_op jit(solution)/shard_map/while/body/eval_jaxpr/ppermute | solution.py:10
  263.4 5.5 %collective-permute-start.1 = (f32[1,2,64]{2,1,0:T(2,128)S(1)}, f32[1,2,64]{2,1,0:T(2,128)S(1)}, u32[]{:S(2)}, u32[]{:S(2)}) collective-permute-start(f32[1,2,64]{2,1,0:T(2,128)S(1)} %constant_dynamic-slice_fusion), channel_id=1, source_target_pairs={{0,1},{1,0},{2,3},{3,2},{4,5},{5,4},{6,7},{7,6},{8,9},{9,8},{10,11... | collective-permute-start | bytes 1544 | tf_op jit(solution)/shard_map/ppermute | solution.py:57
  269.5 6.4 %collective-permute-start.2 = (f32[1,2,64]{2,1,0:T(2,128)S(1)}, f32[1,2,64]{2,1,0:T(2,128)S(1)}, u32[]{:S(2)}, u32[]{:S(2)}) collective-permute-start(f32[1,2,64]{2,1,0:T(2,128)S(1)} %fusion.22), channel_id=1, source_target_pairs={{0,2},{1,3},{2,0},{3,1},{4,6},{5,7},{6,4},{7,5},{8,10},{9,11},{10,... | collective-permute-start | bytes 1544 | tf_op jit(solution)/shard_map/ppermute | solution.py:57
  275.9 9.4 %collective-permute-start.3 = (f32[1,2,64]{2,1,0:T(2,128)S(1)}, f32[1,2,64]{2,1,0:T(2,128)S(1)}, u32[]{:S(2)}, u32[]{:S(2)}) collective-permute-start(f32[1,2,64]{2,1,0:T(2,128)S(1)} %add.163), channel_id=1, source_target_pairs={{0,4},{1,5},{2,6},{3,7},{4,0},{5,1},{6,2},{7,3},{8,12},{9,13},{10,... | collective-permute-start | bytes 1544 | tf_op jit(solution)/shard_map/ppermute | solution.py:57
  285.2 5.5 %collective-permute-start.4 = (f32[1,2,64]{2,1,0:T(2,128)S(1)}, f32[1,2,64]{2,1,0:T(2,128)S(1)}, u32[]{:S(2)}, u32[]{:S(2)}) collective-permute-start(f32[1,2,64]{2,1,0:T(2,128)S(1)} %add.164), channel_id=1, source_target_pairs={{0,8},{1,9},{2,10},{3,11},{4,12},{5,13},{6,14},{7,15},{8,0},{9,1},... | collective-permute-start | bytes 1544 | tf_op jit(solution)/shard_map/ppermute | solution.py:57
  290.7 7.0 %collective-permute-start.5 = (f32[1,2,64]{2,1,0:T(2,128)S(1)}, f32[1,2,64]{2,1,0:T(2,128)S(1)}, u32[]{:S(2)}, u32[]{:S(2)}) collective-permute-start(f32[1,2,64]{2,1,0:T(2,128)S(1)} %add.165), channel_id=1, source_target_pairs={{0,16},{1,17},{2,18},{3,19},{4,20},{5,21},{6,22},{7,23},{8,24},{9,... | collective-permute-start | bytes 1544 | tf_op jit(solution)/shard_map/ppermute | solution.py:57
Sparse Core Ops, SparseCore 0:
  11.2 99.2 all-gather.2
  120.1 217.1 reduce-scatter.1
